TPU v7x, 512 devices: a whole 4x4x16 slice. The times are simulated.
512 devices in a mesh: pipe: 4 (over y), seq: 16 (over z), tensor: 8 (over x, core).
Axes of the slice: x: 4, y: 4, z: 16, core: 2. Of those that a mesh axis runs over, the one named last changes fastest.
Arguments:
- layer_input: bfloat16 [4, 2048, 8192], P('pipe', 'seq', 'tensor'), may hold values from -320 to 320
- conv_out: bfloat16 [4, 2048, 8192], P('pipe', 'seq', 'tensor'), may hold values from -8 to 8
- act_grad: bfloat16 [4, 2048, 8192], P('pipe', 'seq', 'tensor'), may hold values from -6 to 6
- conv_kernel: bfloat16 [4, 4, 8192], P('pipe', None, 'tensor'), may hold values from -3 to 3
- in_proj: bfloat16 [4, 8192, 8192], P('pipe', 'seq', 'tensor'), may hold values from -0.0625 to 0.0625
- sketch_matrix: bfloat16 [4, 8192, 512], P('pipe', 'tensor'), may hold values from -0.0625 to 0.0625
Outputs:
- passed_grad: bfloat16 [4, 2048, 8192], P('pipe', 'tensor', 'seq')
- basis: bfloat16 [4, 8192, 512], P('pipe', 'tensor')
All inputs are finite; a program needn't handle non-finite values.
Results may differ from a plain program's by a relative error of at most 0.017.
Values may be sent and summed in bfloat16 or wider, within the bound.
No kernel may reach another device: no remote copies, remote signals or barrier semaphores. Data moves between devices by JAX's collectives and lax.ppermute only.
A program may use at most 64 MiB of HBM per device.

v0:
```python
import math
import jax
import jax.numpy as jnp
from jax import lax
from jax.sharding import PartitionSpec as P

D = 8192


def passed_along(block, axis, distance):
    devices = range(lax.axis_size(axis))
    route = [(i - distance, i) for i in devices if i - distance in devices]
    return lax.ppermute(block, axis, route)


def shifted(value, axis, by):
    count = lax.axis_size(axis)
    return lax.ppermute(value, axis, [(i, (i + by) % count) for i in range(count)])


def finish_basis(sketch, gram):
    low = jnp.linalg.cholesky(gram)
    ortho_t = lax.linalg.triangular_solve(low, sketch.T, left_side=True, lower=True)
    return (ortho_t.T * math.sqrt(D)).astype(jnp.bfloat16)


def local(layer_input, conv_out, act_grad, conv_kernel, in_proj, sketch_matrix):
    acts = layer_input[0]
    kernel = conv_kernel[0]
    weights = in_proj[0]
    test_matrix = sketch_matrix[0]
    tok_rows = acts.shape[0]
    taps = kernel.shape[0]
    pval = conv_out[0].astype(jnp.float32)
    sig = jax.nn.sigmoid(pval)
    pre_grad = act_grad[0].astype(jnp.float32) * sig * (1.0 + pval * (1.0 - sig))
    ahead = passed_along(pre_grad[: taps - 1], "seq", -1)
    extended = jnp.concatenate([pre_grad, ahead], axis=0)
    total = jnp.zeros(pre_grad.shape, jnp.float32)
    for tap in range(taps):
        total = total + kernel[tap].astype(jnp.float32) * extended[tap : tap + tok_rows]
    in_grad = total.astype(jnp.bfloat16)
    partial_grad = lax.dot_general(
        lax.all_gather(in_grad, "seq", axis=0, tiled=True),
        weights,
        (((1,), (1,)), ((), ())),
        preferred_element_type=jnp.float32,
    )
    input_grad = lax.psum_scatter(
        partial_grad.astype(jnp.bfloat16), "tensor", scatter_dimension=0, tiled=True
    )
    passed = shifted(input_grad, "pipe", -1)
    row_terms = jnp.dot(in_grad, test_matrix, preferred_element_type=jnp.float32)
    sketch_rows = lax.psum(row_terms, "tensor").astype(jnp.bfloat16)
    sketch_part = lax.dot_general(
        acts, sketch_rows, (((0,), (0,)), ((), ())), preferred_element_type=jnp.float32
    )
    sketch = lax.psum(sketch_part, "seq")
    gram_part = jnp.dot(sketch.T, sketch, precision=lax.Precision.HIGHEST)
    gram = lax.psum(gram_part, "tensor")
    basis = finish_basis(sketch, gram)
    return (passed[None], basis[None])


def solution(mesh):
    placed = (
        P("pipe", "seq", "tensor"),
        P("pipe", "seq", "tensor"),
        P("pipe", "seq", "tensor"),
        P("pipe", None, "tensor"),
        P("pipe", "seq", "tensor"),
        P("pipe", "tensor", None),
    )
    return jax.shard_map(
        local,
        mesh=mesh,
        in_specs=placed,
        out_specs=(P("pipe", "tensor", "seq"), P("pipe", "tensor", None)),
        check_vma=False,
    )
```

profile of v0, /device:TPU:26, one launch (start us, length us, event | category | flops | bytes accessed | tf_op | source)
XLA Modules:
  0.0 470.1 jit_solution(17740369245081746752)
XLA Ops:
  7.2 1.4 fusion.30
  8.7 1.3 collective-permute-start
  10.0 0.9 slice_convert_fusion.3
  10.8 3.5 collective-permute-done
  14.9 24.3 %all-reduce.8 = bf16[128,512]{1,0:T(8,128)(2,1)S(1)} all-reduce(f32[128,512]{1,0:T(8,128)S(1)} %fusion.15), channel_id=1, replica_groups=mesh['pipe'=4,'seq'=16,'tensor'=8] {'tensor'}, use_global_device_ids=true, to_apply=%region_1.0 | all-reduce | flops 65536 | bytes 393216 | tf_op jit(solution)/shard_map/psum | solution.py:54
  39.2 1.8 convolution_bitcast_fusion
  41.0 149.0 %all-reduce.5.cloned.1.call-done = f32[1024,512]{0,1:T(8,128)} async-done(((f32[1024,512]{0,1:T(8,128)}), f32[1024,512]{0,1:T(8,128)}) %all-reduce.5.cloned.1.call-update) | async-done | bytes 2097168 | tf_op jit(solution)/shard_map/psum | solution.py:58
  190.0 6.7 %fusion.56 = f32[512,512]{0,1:T(8,128)} fusion(f32[1024,512]{0,1:T(8,128)} %all-reduce.5.cloned.1.call-done), kind=kOutput, calls=%fused_computation.103 | convolution fusion | flops 3221225472 | bytes 3145728 | tf_op jit(solution)/shard_map/dot_general | solution.py:59
  196.8 0.7 all-gather.2.cloned.1.call-update
  198.0 70.5 %all-reduce.7.cloned.1.call-done = f32[512,512]{0,1:T(8,128)} async-done(((f32[512,512]{0,1:T(8,128)}), f32[512,512]{0,1:T(8,128)}) %all-reduce.7.cloned.1.call-update) | async-done | bytes 1048592 | tf_op jit(solution)/shard_map/psum | solution.py:60
  268.5 1.6 copy.9
  270.4 1.0 copy-done.7
  271.4 11.7 %cholesky.104 = f32[128,128]{1,0:T(8,128)S(1)} custom-call(f32[128,128]{1,0:T(8,128)S(1)} %cholesky.266), custom_call_target="Cholesky" | custom-call | tf_op jit(solution)/shard_map/jit(cholesky)/cholesky | solution.py:22
  283.3 9.8 %custom-call.30 = f32[1,128,128]{1,2,0:T(8,128)S(1)} custom-call(f32[1,128,128]{2,1,0:T(8,128)S(1)} %get-tuple-element.31), custom_call_target="InvertDiagBlocksLowerTriangular" | custom-call | tf_op jit(solution)/shard_map/jit(cholesky)/cholesky | solution.py:22
  293.1 1.2 constant_dynamic-update-slice_fusion.3
  294.4 1.3 convolution_subtract_fusion.2
  295.6 11.7 %cholesky.217 = f32[128,128]{1,0:T(8,128)S(1)} custom-call(f32[128,128]{1,0:T(8,128)S(1)} %cholesky.270), custom_call_target="Cholesky" | custom-call | tf_op jit(solution)/shard_map/jit(cholesky)/cholesky | solution.py:22
  307.4 10.0 %custom-call.31 = f32[1,128,128]{1,2,0:T(8,128)S(1)} custom-call(f32[1,128,128]{2,1,0:T(8,128)S(1)} %get-tuple-element.28), custom_call_target="InvertDiagBlocksLowerTriangular" | custom-call | tf_op jit(solution)/shard_map/jit(cholesky)/cholesky | solution.py:22
  317.6 1.4 convolution_subtract_fusion.3
  319.1 11.7 %cholesky.238 = f32[128,128]{1,0:T(8,128)S(1)} custom-call(f32[128,128]{1,0:T(8,128)S(1)} %cholesky.275), custom_call_target="Cholesky" | custom-call | tf_op jit(solution)/shard_map/jit(cholesky)/cholesky | solution.py:22
  330.8 21.4 %all-gather.2.cloned.1.call-done = bf16[2048,1024]{1,0:T(8,128)(2,1)} async-done(((bf16[128,1024]{1,0:T(8,128)(2,1)}), bf16[2048,1024]{1,0:T(8,128)(2,1)}) %all-gather.2.cloned.1.call-update) | async-done | bytes 4194320 | tf_op jit(solution)/shard_map/all_gather | solution.py:44
  352.2 5.9 %convolution_convert_fusion = bf16[2048,512]{1,0:T(8,128)(2,1)} fusion(bf16[2048,1024]{1,0:T(8,128)(2,1)} %all-gather.2.cloned.1.call-done, bf16[1,512,1024]{2,1,0:T(8,128)(2,1)S(1)} %copy-done), kind=kOutput, calls=%fused_computation.2 | convolution fusion | flops 2148532224 | bytes 7340032 | tf_op jit(solution)/shard_map/dot_general | solution.py:43
  358.1 0.6 select_reduce_fusion.1
  358.8 9.8 %custom-call.32 = f32[1,128,128]{1,2,0:T(8,128)S(1)} custom-call(f32[1,128,128]{2,1,0:T(8,128)S(1)} %get-tuple-element.25), custom_call_target="InvertDiagBlocksLowerTriangular" | custom-call | tf_op jit(solution)/shard_map/jit(cholesky)/cholesky | solution.py:22
  368.6 0.8 convolution_dynamic-update-slice_fusion.1
  369.4 1.5 convolution_subtract_fusion.4
  370.9 11.9 %cholesky.255 = f32[128,128]{1,0:T(8,128)S(1)} custom-call(f32[128,128]{1,0:T(8,128)S(1)} %convolution_subtract_fusion.4), custom_call_target="Cholesky" | custom-call | tf_op jit(solution)/shard_map/jit(cholesky)/cholesky | solution.py:22
  382.8 0.6 compare_reduce_fusion.2
  384.8 0.6 compare_reduce_fusion.1
  386.1 0.6 select_reduce_fusion
  386.7 0.6 compare_reduce_fusion
  388.0 2.3 select_select_fusion
  390.3 13.6 %while.1 = (s32[]{:T(128)}, f32[512,512]{1,0:T(8,128)}, s32[4,2]{0,1:T(2,128)S(1)}, f32[4,128,128]{2,1,0:T(8,128)}, s32[]{:T(128)}) while((s32[]{:T(128)}, f32[512,512]{1,0:T(8,128)}, s32[4,2]{0,1:T(2,128)S(1)}, f32[4,128,128]{2,1,0:T(8,128)}, s32[]{:T(128)}) %tuple.35), condition=%wide.while_cond, body=%wide.while_body.sunk | while | flops 2 | bytes 132205 | solution.py:23
  390.9 2.8 bitcast_dynamic-update-slice_fusion.2
  394.4 2.8 bitcast_dynamic-update-slice_fusion.2
  397.8 2.8 bitcast_dynamic-update-slice_fusion.2
  401.2 2.8 bitcast_dynamic-update-slice_fusion.2
  404.0 40.1 %custom-call.33 = f32[4,128,128]{1,2,0:T(8,128)S(1)} custom-call(f32[4,128,128]{2,1,0:T(8,128)} %get-tuple-element.9), custom_call_target="InvertDiagBlocksLowerTriangular" | custom-call | tf_op jit(solution)/shard_map/triangular_solve | solution.py:23
  444.8 1.5 convolution_subtract_fusion.1
  446.9 1.8 convolution_subtract_fusion
  449.4 0.8 copy-done.5
  450.1 2.8 fusion.7
  453.0 2.4 collective-permute-start.1
  455.4 1.7 fusion.44
  457.1 1.6 fusion.10
  458.8 1.3 copy.10
  460.1 2.6 collective-permute-done.1
  462.7 0.7 copy.32
  (53 shorter events, 6.3 us)
Async XLA Ops:
  7.2 345.0 %copy-start = (bf16[1,512,1024]{2,1,0:T(8,128)(2,1)S(1)}, bf16[1,512,1024]{2,1,0:T(8,128)(2,1)}, u32[]{:S(2)}) copy-start(bf16[1,512,1024]{2,1,0:T(8,128)(2,1)} %param.10) | copy-start | bytes 3145732
  7.2 7.4 %copy-start.9 = (bf16[1,1024,512]{2,1,0:T(8,128)(2,1)S(1)}, bf16[1,1024,512]{2,1,0:T(8,128)(2,1)}, u32[]{:S(2)}) copy-start(bf16[1,1024,512]{2,1,0:T(8,128)(2,1)} %param.11) | copy-start | bytes 3145732
  7.2 32.0 %copy-start.10 = (bf16[1,128,1024]{2,1,0:T(8,128)(2,1)S(1)}, bf16[1,128,1024]{2,1,0:T(8,128)(2,1)}, u32[]{:S(2)}) copy-start(bf16[1,128,1024]{2,1,0:T(8,128)(2,1)} %param.6) | copy-start | bytes 786436
  7.2 182.8 %all-reduce.5.cloned.1.call-start = ((), (), s32[]{:S(2)}) async-start(), calls=%async_computation.3 | async-start | bytes 4194304 | tf_op jit(solution)/shard_map/psum | solution.py:58
  8.7 5.6 %collective-permute-start = (f32[3,1024]{1,0:T(4,128)S(1)}, f32[3,1024]{1,0:T(4,128)S(1)}, u32[]{:S(2)}, u32[]{:S(2)}) collective-permute-start(f32[3,1024]{1,0:T(4,128)S(1)} %slice.150), channel_id=1, source_target_pairs={{8,0},{16,8},{24,16},{32,24},{40,32},{48,40},{56,48},{64,56},{72,6... | collective-permute-start | bytes 36872 | tf_op jit(solution)/shard_map/ppermute | solution.py:13
  14.5 26.4 %copy-start.8 = (bf16[128,1024]{1,0:T(8,128)(2,1)}, bf16[128,1024]{1,0:T(8,128)(2,1)S(1)}, u32[]{:S(2)}) copy-start(bf16[128,1024]{1,0:T(8,128)(2,1)S(1)} %fusion.22) | copy-start | bytes 786436
  41.0 227.5 %all-reduce.7.cloned.1.call-start = ((), (), s32[]{:S(2)}) async-start(), calls=%async_computation.4 | async-start | bytes 2097152 | tf_op jit(solution)/shard_map/psum | solution.py:60
  196.8 155.4 %all-gather.2.cloned.1.call-start = ((), (), s32[]{:S(2)}) async-start(), calls=%async_computation.1 | async-start | bytes 4456448 | tf_op jit(solution)/shard_map/all_gather | solution.py:44
  197.5 255.5 %reduce-scatter.2.cloned.1.call-start = ((), (), s32[]{:S(2)}) async-start(), calls=%async_computation.2 | async-start | bytes 2359296 | tf_op jit(solution)/shard_map/reduce_scatter | solution.py:49
  268.5 1.7 copy-start.6
  270.4 1.0 copy-start.7
  317.6 40.5 %copy-start.4 = (f32[512,512]{1,0:T(8,128)}, f32[512,512]{1,0:T(8,128)S(1)}, u32[]{:S(2)}) copy-start(f32[512,512]{1,0:T(8,128)S(1)} %convolution_dynamic-update-slice_fusion) | copy-start | bytes 3145732
  358.1 86.0 %copy-start.1 = (f32[1024,512]{0,1:T(8,128)S(1)}, f32[1024,512]{0,1:T(8,128)}, u32[]{:S(2)}) copy-start(f32[1024,512]{0,1:T(8,128)} %all-reduce.5.cloned.1.call-done) | copy-start | bytes 6291460
  444.8 4.6 copy-start.2
  446.9 2.4 copy-start.3
  449.3 0.8 copy-start.5
  453.0 9.7 %collective-permute-start.1 = (bf16[256,512]{1,0:T(8,128)(2,1)}, bf16[256,512]{1,0:T(8,128)(2,1)S(1)}, u32[]{:S(2)}, u32[]{:S(2)}) collective-permute-start(bf16[256,512]{1,0:T(8,128)(2,1)} %reduce-scatter.2.cloned.1.call-done), channel_id=1, source_target_pairs={{0,384},{128,0},{256,128},{384,256},{1,385},{129,1},{257,129},{385... | collective-permute-start | bytes 786440 | tf_op jit(solution)/shard_map/ppermute | solution.py:18
Sparse Core Ops, SparseCore 0:
  41.1 148.8 all-reduce.4
  196.9 71.6 all-reduce.6
  271.2 80.9 all-gather.1
  358.2 33.6 reduce-scatter.1
where the time goes:
time: 475 us; the launch traced here: 470 us
  waiting for transfers between devices  248 us (52%)
  other arithmetic  127 us (27%)
  matrix products  30.9 us (7%)
  blocking collectives  24.3 us (5%)
  local copies, waits for them, and re-layouts  19.3 us (4%)
  between operations  17 us (4%)
    psum x1, waiting for transfers between devices, local(): sketch = lax.psum(sketch_part, 'seq')  149 us
    another operation x14, other arithmetic, finish_basis(): low = jnp.linalg.cholesky(gram)  79.9 us
    psum x1, waiting for transfers between devices, local(): gram = lax.psum(gram_part, 'tensor')  70.5 us
    another operation x3, other arithmetic, finish_basis(): lax.linalg.triangular_solve(low, sketch.T, left_side=True, lower=True)  42.5 us
    psum x1, blocking collectives, local(): sketch_rows = lax.psum(row_terms, 'tensor').astype(jnp.bfloat16)  24.3 us
    all_gather x1, waiting for transfers between devices, local(): lax.all_gather(in_grad, 'seq', axis=0, tiled=True)  21.4 us
    another operation x12, local copies, waits for them, and re-layouts  13.6 us
    another operation x7, matrix products, finish_basis(): lax.linalg.triangular_solve(low, sketch.T, left_side=True, lower=True)  9.66 us
  transfers between devices with their start and end apart: 6, of which 5 were waited for; matrix products, arithmetic and copies ran while one was open for 34% of the time, Pallas kernels for 0%

commit v1 on v0

--- a/solution.py
+++ b/solution.py
@@ -5,6 +5,13 @@
 from jax.sharding import PartitionSpec as P
 
 D = 8192
+
+
+def swapped_in(value, axis, dim):
+    peers = lax.axis_size(axis)
+    blocks = jnp.stack([value for _ in range(peers)])
+    blocks = lax.all_to_all(blocks, axis, split_axis=0, concat_axis=0)
+    return jnp.concatenate(blocks, axis=dim)
 
 
 def passed_along(block, axis, distance):
@@ -41,7 +48,7 @@
         total = total + kernel[tap].astype(jnp.float32) * extended[tap : tap + tok_rows]
     in_grad = total.astype(jnp.bfloat16)
     partial_grad = lax.dot_general(
-        lax.all_gather(in_grad, "seq", axis=0, tiled=True),
+        swapped_in(in_grad, "seq", 0),
         weights,
         (((1,), (1,)), ((), ())),
         preferred_element_type=jnp.float32,

time: 475 us -> 573 us (1.21)
  the two profiles are of different devices: /device:TPU:26 before, /device:TPU:31 now
where the time goes in v1:
time: 573 us; the launch traced here: 568 us
  waiting for transfers between devices  324 us (57%)
  other arithmetic  127 us (22%)
  matrix products  30.8 us (5%)
  blocking collectives  27.4 us (5%)
  local copies, waits for them, and re-layouts  22.1 us (4%)
  starting transfers between devices  19.2 us (3%)
  between operations  16.9 us (3%)
    psum x1, waiting for transfers between devices, local(): sketch = lax.psum(sketch_part, 'seq')  236 us
    psum x1, waiting for transfers between devices, local(): gram = lax.psum(gram_part, 'tensor')  81 us
    another operation x14, other arithmetic, finish_basis(): low = jnp.linalg.cholesky(gram)  79.9 us
    another operation x3, other arithmetic, finish_basis(): lax.linalg.triangular_solve(low, sketch.T, left_side=True, lower=True)  42.5 us
    psum x1, blocking collectives, local(): sketch_rows = lax.psum(row_terms, 'tensor').astype(jnp.bfloat16)  27.4 us
    all_to_all x1, starting transfers between devices, swapped_in(): blocks = lax.all_to_all(blocks, axis, split_axis=0, concat_axis=0)  14.9 us
    another operation x12, local copies, waits for them, and re-layouts  14 us
  transfers between devices with their start and end apart: 6, of which 4 were waited for; matrix products, arithmetic and copies ran while one was open for 29% of the time, Pallas kernels for 0%

profile of v1, /device:TPU:31, one launch (start us, length us, event | category | flops | bytes accessed | tf_op | source)
XLA Modules:
  0.0 567.5 jit_solution(11140465451942483790)
XLA Ops:
  7.2 1.3 fusion.30
  8.5 1.3 collective-permute-start
  9.8 0.9 slice_convert_fusion.3
  10.7 2.5 collective-permute-done
  13.4 2.5 stack.2
  15.9 14.9 %all-to-all-start = ((bf16[16,128,1024]{2,1,0:T(8,128)(2,1)}), bf16[16,128,1024]{2,1,0:T(8,128)(2,1)}, u32[]{:S(2)}, u32[]{:S(2)}) async-start(bf16[16,128,1024]{2,1,0:T(8,128)(2,1)} %stack.2), calls=%async_computation | async-start | bytes 8388608 | tf_op jit(solution)/shard_map/all_to_all | solution.py:13
  31.2 27.4 %all-reduce.8 = bf16[128,512]{1,0:T(8,128)(2,1)S(1)} all-reduce(f32[128,512]{1,0:T(8,128)S(1)} %fusion.15), channel_id=1, replica_groups=mesh['pipe'=4,'seq'=16,'tensor'=8] {'tensor'}, use_global_device_ids=true, to_apply=%region_1.0 | all-reduce | flops 65536 | bytes 393216 | tf_op jit(solution)/shard_map/psum | solution.py:61
  58.7 1.8 convolution_bitcast_fusion
  60.5 236.5 %all-reduce.5.cloned.1.call-done = f32[1024,512]{0,1:T(8,128)} async-done(((f32[1024,512]{0,1:T(8,128)}), f32[1024,512]{0,1:T(8,128)}) %all-reduce.5.cloned.1.call-update) | async-done | bytes 2097168 | tf_op jit(solution)/shard_map/psum | solution.py:65
  297.0 6.7 %fusion.56 = f32[512,512]{0,1:T(8,128)} fusion(f32[1024,512]{0,1:T(8,128)} %all-reduce.5.cloned.1.call-done), kind=kOutput, calls=%fused_computation.103 | convolution fusion | flops 3221225472 | bytes 3145728 | tf_op jit(solution)/shard_map/dot_general | solution.py:66
  304.3 81.0 %all-reduce.7.cloned.1.call-done = f32[512,512]{0,1:T(8,128)} async-done(((f32[512,512]{0,1:T(8,128)}), f32[512,512]{0,1:T(8,128)}) %all-reduce.7.cloned.1.call-update) | async-done | bytes 1048592 | tf_op jit(solution)/shard_map/psum | solution.py:67
  385.3 1.6 copy.9
  387.2 1.0 copy-done.7
  388.2 11.7 %cholesky.104 = f32[128,128]{1,0:T(8,128)S(1)} custom-call(f32[128,128]{1,0:T(8,128)S(1)} %cholesky.266), custom_call_target="Cholesky" | custom-call | tf_op jit(solution)/shard_map/jit(cholesky)/cholesky | solution.py:29
  400.0 9.8 %custom-call.30 = f32[1,128,128]{1,2,0:T(8,128)S(1)} custom-call(f32[1,128,128]{2,1,0:T(8,128)S(1)} %get-tuple-element.31), custom_call_target="InvertDiagBlocksLowerTriangular" | custom-call | tf_op jit(solution)/shard_map/jit(cholesky)/cholesky | solution.py:29
  409.9 1.2 constant_dynamic-update-slice_fusion.3
  411.1 1.3 convolution_subtract_fusion.2
  412.4 11.7 %cholesky.217 = f32[128,128]{1,0:T(8,128)S(1)} custom-call(f32[128,128]{1,0:T(8,128)S(1)} %cholesky.270), custom_call_target="Cholesky" | custom-call | tf_op jit(solution)/shard_map/jit(cholesky)/cholesky | solution.py:29
  424.1 10.0 %custom-call.31 = f32[1,128,128]{1,2,0:T(8,128)S(1)} custom-call(f32[1,128,128]{2,1,0:T(8,128)S(1)} %get-tuple-element.28), custom_call_target="InvertDiagBlocksLowerTriangular" | custom-call | tf_op jit(solution)/shard_map/jit(cholesky)/cholesky | solution.py:29
  434.4 1.4 convolution_subtract_fusion.3
  435.8 11.7 %cholesky.238 = f32[128,128]{1,0:T(8,128)S(1)} custom-call(f32[128,128]{1,0:T(8,128)S(1)} %cholesky.275), custom_call_target="Cholesky" | custom-call | tf_op jit(solution)/shard_map/jit(cholesky)/cholesky | solution.py:29
  447.6 5.9 %convolution_convert_fusion = bf16[2048,512]{1,0:T(8,128)(2,1)} fusion(bf16[2048,1024]{1,0:T(8,128)(2,1)} %bitcast.7, bf16[1,512,1024]{2,1,0:T(8,128)(2,1)S(1)} %copy-done), kind=kOutput, calls=%fused_computation.2 | convolution fusion | flops 2148532224 | bytes 7340032 | tf_op jit(solution)/shard_map/dot_general | solution.py:50
  453.5 0.7 select_reduce_fusion.1
  454.2 9.8 %custom-call.32 = f32[1,128,128]{1,2,0:T(8,128)S(1)} custom-call(f32[1,128,128]{2,1,0:T(8,128)S(1)} %get-tuple-element.25), custom_call_target="InvertDiagBlocksLowerTriangular" | custom-call | tf_op jit(solution)/shard_map/jit(cholesky)/cholesky | solution.py:29
  464.0 0.8 convolution_dynamic-update-slice_fusion.1
  464.8 1.4 convolution_subtract_fusion.4
  466.2 11.9 %cholesky.255 = f32[128,128]{1,0:T(8,128)S(1)} custom-call(f32[128,128]{1,0:T(8,128)S(1)} %convolution_subtract_fusion.4), custom_call_target="Cholesky" | custom-call | tf_op jit(solution)/shard_map/jit(cholesky)/cholesky | solution.py:29
  478.1 0.6 compare_reduce_fusion.2
  480.0 0.6 compare_reduce_fusion.1
  481.3 0.6 select_reduce_fusion
  481.9 0.6 compare_reduce_fusion
  483.2 2.3 select_select_fusion
  485.5 14.0 %while.1 = (s32[]{:T(128)}, f32[512,512]{1,0:T(8,128)}, s32[4,2]{0,1:T(2,128)S(1)}, f32[4,128,128]{2,1,0:T(8,128)}, s32[]{:T(128)}) while((s32[]{:T(128)}, f32[512,512]{1,0:T(8,128)}, s32[4,2]{0,1:T(2,128)S(1)}, f32[4,128,128]{2,1,0:T(8,128)}, s32[]{:T(128)}) %tuple.35), condition=%wide.while_cond, body=%wide.while_body.sunk | while | flops 2 | bytes 132205 | solution.py:30
  486.2 2.9 bitcast_dynamic-update-slice_fusion.2
  489.7 2.9 bitcast_dynamic-update-slice_fusion.2
  493.2 2.9 bitcast_dynamic-update-slice_fusion.2
  496.7 2.8 bitcast_dynamic-update-slice_fusion.2
  499.5 40.1 %custom-call.33 = f32[4,128,128]{1,2,0:T(8,128)S(1)} custom-call(f32[4,128,128]{2,1,0:T(8,128)} %get-tuple-element.9), custom_call_target="InvertDiagBlocksLowerTriangular" | custom-call | tf_op jit(solution)/shard_map/triangular_solve | solution.py:30
  540.3 1.5 convolution_subtract_fusion.1
  542.4 1.8 convolution_subtract_fusion
  544.9 0.8 copy-done.5
  545.7 2.8 fusion.7
  548.5 2.4 collective-permute-start.1
  551.0 1.7 fusion.44
  552.6 1.6 fusion.10
  554.3 1.3 copy.10
  555.6 4.5 collective-permute-done.1
  560.1 0.7 copy.32
  (51 shorter events, 6.5 us)
Async XLA Ops:
  7.2 440.4 %copy-start = (bf16[1,512,1024]{2,1,0:T(8,128)(2,1)S(1)}, bf16[1,512,1024]{2,1,0:T(8,128)(2,1)}, u32[]{:S(2)}) copy-start(bf16[1,512,1024]{2,1,0:T(8,128)(2,1)} %param.10) | copy-start | bytes 3145732
  8.5 4.7 collective-permute-start
  15.9 15.0 %copy-start.8 = (bf16[1,1024,512]{2,1,0:T(8,128)(2,1)S(1)}, bf16[1,1024,512]{2,1,0:T(8,128)(2,1)}, u32[]{:S(2)}) copy-start(bf16[1,1024,512]{2,1,0:T(8,128)(2,1)} %param.11) | copy-start | bytes 3145732
  15.9 431.6 %all-to-all-start = ((bf16[16,128,1024]{2,1,0:T(8,128)(2,1)}), bf16[16,128,1024]{2,1,0:T(8,128)(2,1)}, u32[]{:S(2)}, u32[]{:S(2)}) async-start(bf16[16,128,1024]{2,1,0:T(8,128)(2,1)} %stack.2), calls=%async_computation | async-start | bytes 8388608 | tf_op jit(solution)/shard_map/all_to_all | solution.py:13
  30.9 27.8 %copy-start.9 = (bf16[1,128,1024]{2,1,0:T(8,128)(2,1)S(1)}, bf16[1,128,1024]{2,1,0:T(8,128)(2,1)}, u32[]{:S(2)}) copy-start(bf16[1,128,1024]{2,1,0:T(8,128)(2,1)} %param.6) | copy-start | bytes 786436
  30.9 266.2 %all-reduce.5.cloned.1.call-start = ((), (), s32[]{:S(2)}) async-start(), calls=%async_computation.3 | async-start | bytes 4194304 | tf_op jit(solution)/shard_map/psum | solution.py:65
  60.5 324.8 %all-reduce.7.cloned.1.call-start = ((), (), s32[]{:S(2)}) async-start(), calls=%async_computation.4 | async-start | bytes 2097152 | tf_op jit(solution)/shard_map/psum | solution.py:67
  303.8 244.7 %reduce-scatter.2.cloned.1.call-start = ((), (), s32[]{:S(2)}) async-start(), calls=%async_computation.2 | async-start | bytes 2359296 | tf_op jit(solution)/shard_map/reduce_scatter | solution.py:56
  385.3 1.7 copy-start.6
  387.2 1.0 copy-start.7
  434.4 19.1 %copy-start.4 = (f32[512,512]{1,0:T(8,128)}, f32[512,512]{1,0:T(8,128)S(1)}, u32[]{:S(2)}) copy-start(f32[512,512]{1,0:T(8,128)S(1)} %convolution_dynamic-update-slice_fusion) | copy-start | bytes 3145732
  453.5 86.1 %copy-start.1 = (f32[1024,512]{0,1:T(8,128)S(1)}, f32[1024,512]{0,1:T(8,128)}, u32[]{:S(2)}) copy-start(f32[1024,512]{0,1:T(8,128)} %all-reduce.5.cloned.1.call-done) | copy-start | bytes 6291460
  540.3 4.6 copy-start.2
  542.4 2.4 copy-start.3
  544.9 0.8 copy-start.5
  548.5 11.6 %collective-permute-start.1 = (bf16[256,512]{1,0:T(8,128)(2,1)}, bf16[256,512]{1,0:T(8,128)(2,1)S(1)}, u32[]{:S(2)}, u32[]{:S(2)}) collective-permute-start(bf16[256,512]{1,0:T(8,128)(2,1)} %reduce-scatter.2.cloned.1.call-done), channel_id=1, source_target_pairs={{0,384},{128,0},{256,128},{384,256},{1,385},{129,1},{257,129},{385... | collective-permute-start | bytes 786440 | tf_op jit(solution)/shard_map/ppermute | solution.py:25
Sparse Core Ops, SparseCore 0:
  60.6 236.3 all-reduce.4
  303.9 81.3 all-reduce.6
  453.6 40.2 reduce-scatter.1
